TPU v7x, 256 devices: a whole 4x4x8 slice. The times are simulated.
256 devices in a mesh: rows: 4 (over y), seq: 64 (over z, x, core).
Axes of the slice: x: 4, y: 4, z: 8, core: 2. Of those that a mesh axis runs over, the one named last changes fastest.
Arguments:
- rollout_query: bfloat16 [32768, 24576], P(('rows', 'seq')), may hold values from -210 to 210
- rollout_latent: bfloat16 [32768, 576], P(('rows', 'seq')), may hold values from -40 to 40
- trainer_row: int32 [4, 8192], P(None, 'seq'), may hold values from 0 to 3, as said below
- segment_ids: int32 [4, 8192], P('rows'), may hold values from 0 to 63, never falling along the last dimension, each value on 1 to 256 neighbouring positions
- kv_gain: float32 [512], replicated, may hold values from 0.1 to 1.9
- key_up: bfloat16 [512, 16384], P(None, 'seq'), may hold values from -0.25 to 0.25
- value_up: bfloat16 [512, 16384], P(None, 'seq'), may hold values from -0.25 to 0.25
Outputs:
- attended: bfloat16 [32768, 16384], P(('rows', 'seq'))
Inputs may be any that keep to these rules, and one draw needn't show every extreme that they name: `trainer_row`: for each seq index, each trainer row receives exactly 128 tokens from the 4 rollout devices of that seq index; at most 48 tokens go from one rollout device to one trainer row, and this bound is reached for every seq index. `segment_ids`: each response occupies at most 256 consecutive positions of a packed row.
All inputs are finite; a program needn't handle non-finite values.
Results may differ from a plain program's by a relative error of at most 0.0068.
Values may be sent and summed in bfloat16 or wider, within the bound.
A program may use at most 192 MiB of HBM per device.

v0:
```python
import math

import jax
import jax.numpy as jnp
from jax import lax
from jax.sharding import PartitionSpec as P

HEADS = 128
QK_NOPE = 128
QK_ROPE = 64
V_HEAD = 128
LATENT = 512
SEG_MOST = 256


def attend_rows(queries, keys, values, segment_row):
    span = SEG_MOST
    total = queries.shape[0]
    block_rows = min(512, total)
    heads_here = queries.shape[1]
    scale = 1.0 / math.sqrt(QK_NOPE + QK_ROPE)
    padded_keys = jnp.concatenate(
        [jnp.zeros((span, heads_here, keys.shape[2]), keys.dtype), keys], 0
    )
    padded_values = jnp.concatenate(
        [jnp.zeros((span, heads_here, values.shape[2]), values.dtype), values], 0
    )
    padded_segments = jnp.concatenate([jnp.full((span,), -1, jnp.int32), segment_row], 0)

    def one_block(block_index):
        begin_row = block_index * block_rows
        query_block = lax.dynamic_slice_in_dim(queries, begin_row, block_rows, 0)
        key_block = lax.dynamic_slice_in_dim(padded_keys, begin_row, block_rows + span, 0)
        value_block = lax.dynamic_slice_in_dim(padded_values, begin_row, block_rows + span, 0)
        query_segments = lax.dynamic_slice_in_dim(padded_segments, begin_row + span, block_rows, 0)
        key_segments = lax.dynamic_slice_in_dim(padded_segments, begin_row, block_rows + span, 0)
        scores = (
            jnp.einsum("qhd,khd->hqk", query_block, key_block, preferred_element_type=jnp.float32)
            * scale
        )
        query_pos = begin_row + jnp.arange(block_rows, dtype=jnp.int32)
        key_pos = begin_row - span + jnp.arange(block_rows + span, dtype=jnp.int32)
        allowed = (query_segments[:, None] == key_segments[None, :]) & (
            key_pos[None, :] <= query_pos[:, None]
        )
        scores = jnp.where(allowed[None], scores, -1e30)
        top_score = jnp.max(scores, axis=-1, keepdims=True)
        weights = jnp.exp(scores - top_score)
        weights = (weights / jnp.sum(weights, axis=-1, keepdims=True)).astype(jnp.bfloat16)
        mixed = jnp.einsum("hqk,khd->qhd", weights, value_block, preferred_element_type=jnp.float32)
        return mixed.astype(jnp.bfloat16)

    blocks = lax.map(one_block, jnp.arange(total // block_rows, dtype=jnp.int32))
    return blocks.reshape(total, heads_here, values.shape[2])


def reshard_both(query_buffer, latent_buffer):
    return (
        lax.all_to_all(query_buffer, "rows", split_axis=0, concat_axis=0, tiled=True),
        lax.all_to_all(latent_buffer, "rows", split_axis=0, concat_axis=0, tiled=True),
    )


def normalize_rows(packed_latent, kv_gain):
    latent_part = packed_latent[:, :LATENT].astype(jnp.float32)
    inverse_rms = lax.rsqrt(jnp.mean(latent_part * latent_part, axis=-1, keepdims=True) + 1e-06)
    normed = (latent_part * inverse_rms * kv_gain).astype(jnp.bfloat16)
    return jnp.concatenate([normed, packed_latent[:, LATENT:]], 1)


def local(rollout_query, rollout_latent, trainer_row, segment_ids, kv_gain, key_up, value_up):
    num_rows = lax.axis_size("rows")
    own_row = lax.axis_index("rows")
    num_tokens = rollout_query.shape[0]
    capacity = num_tokens // num_rows + num_tokens // 8
    row_ids = jnp.arange(num_rows, dtype=jnp.int32)
    targets = lax.dynamic_index_in_dim(trainer_row, own_row, 0, keepdims=False)
    one_hot = (targets[:, None] == row_ids[None, :]).astype(jnp.int32)
    rank_within = jnp.sum((jnp.cumsum(one_hot, axis=0) - 1) * one_hot, axis=1)
    slot_index = targets * capacity + rank_within
    latent_buffer = (
        jnp.zeros((num_rows * capacity, rollout_latent.shape[1]), jnp.bfloat16)
        .at[slot_index]
        .set(rollout_latent)
    )
    arrivals = jnp.sum((trainer_row == own_row).astype(jnp.int32), axis=1)
    block_ends = jnp.cumsum(arrivals)
    block_begins = block_ends - arrivals
    positions = jnp.arange(num_tokens, dtype=jnp.int32)
    source_block = jnp.sum((positions[:, None] >= block_ends[None, :]).astype(jnp.int32), axis=1)
    block_begin = jnp.sum(
        jnp.where(source_block[:, None] == row_ids[None, :], block_begins[None, :], 0), axis=1
    )
    take_index = source_block * capacity + positions - block_begin
    group_count = lax.axis_size("seq")
    head_width = QK_NOPE + QK_ROPE
    segment_row = segment_ids[0]
    local_heads = key_up.shape[1] // QK_NOPE
    row_length = num_tokens * group_count
    query_buffer = (
        jnp.zeros((num_rows * capacity, rollout_query.shape[1]), jnp.bfloat16)
        .at[slot_index]
        .set(rollout_query)
    )
    query_in, latent_in = reshard_both(query_buffer, latent_buffer)
    packed_query = query_in[take_index]
    packed_latent = latent_in[take_index]
    head_query = lax.all_to_all(
        packed_query.reshape(num_tokens, group_count, local_heads * head_width),
        "seq",
        split_axis=1,
        concat_axis=0,
        tiled=True,
    )
    head_query = head_query.reshape(row_length, local_heads, head_width)
    latent_norm = normalize_rows(packed_latent, kv_gain)
    latent_piece = lax.all_gather(latent_norm, "seq", axis=0, tiled=True)
    latent_cols = latent_piece[:, :LATENT]
    key_nope = jnp.dot(latent_cols, key_up, preferred_element_type=jnp.float32).astype(jnp.bfloat16)
    value_rows = jnp.dot(latent_cols, value_up, preferred_element_type=jnp.float32).astype(
        jnp.bfloat16
    )
    expanded = jnp.concatenate([key_nope, value_rows, latent_piece[:, LATENT:]], 1)
    key_nope = expanded[:, : local_heads * QK_NOPE].reshape(row_length, local_heads, QK_NOPE)
    value_rows = expanded[:, local_heads * QK_NOPE : local_heads * (QK_NOPE + V_HEAD)].reshape(
        row_length, local_heads, V_HEAD
    )
    rotary_key = expanded[:, local_heads * (QK_NOPE + V_HEAD) :]
    rotary_all = jnp.broadcast_to(rotary_key[:, None, :], (row_length, local_heads, QK_ROPE))
    keys = jnp.concatenate([key_nope, rotary_all], 2)
    head_out = attend_rows(head_query, keys, value_rows, segment_row)
    returned = lax.all_to_all(
        head_out.reshape(group_count, num_tokens, 1, local_heads * V_HEAD),
        "seq",
        split_axis=0,
        concat_axis=2,
        tiled=True,
    )
    return returned.reshape(num_tokens, HEADS * V_HEAD)


def solution(mesh):
    placed = (
        P(("rows", "seq"), None),
        P(("rows", "seq"), None),
        P(None, "seq"),
        P("rows", None),
        P(),
        P(None, "seq"),
        P(None, "seq"),
    )
    return jax.shard_map(
        local, mesh=mesh, in_specs=placed, out_specs=P(("rows", "seq"), None), check_vma=False
    )
```

profile of v0, /device:TPU:1, one launch (start us, length us, event | category | flops | bytes accessed | tf_op | source)
XLA Modules:
  0.0 604.2 jit_solution(11414972993865848027)
XLA Ops:
  9.5 1.8 scatter_custom_fusion
  11.2 5.0 all-to-all-start
  17.5 4.2 all-to-all-done
  24.2 16.0 %scatter_custom_fusion.1 = bf16[192,24576]{1,0:T(8,128)(2,1)} fusion(s32[128]{0:T(128)S(1)} %fusion.30, bf16[128,24576]{1,0:T(8,128)(2,1)} %param.9, bf16[]{:T(256)} %constant.96.clone.1), kind=kCustom, calls=%fused_computation.36 | custom fusion | bytes 9437696 | tf_op jit(solution)/shard_map/scatter | solution.py:103
  40.3 110.0 %all_to_all.54 = bf16[4,48,24576]{2,1,0:T(8,128)(2,1)} all-to-all(bf16[4,48,24576]{2,1,0:T(8,128)(2,1)} %bitcast.64), channel_id=1, replica_groups=mesh['rows'=4,'seq'=64] {'rows'}, dimensions={0} | all-to-all | bytes 18874368 | tf_op jit(solution)/shard_map/all_to_all | solution.py:59
  150.2 17.5 %gather_fusion.1 = bf16[128,24576]{1,0:T(8,128)(2,1)} fusion(bf16[192,24576]{1,0:T(8,128)(2,1)} %bitcast.63, s32[1024]{0:T(1024)S(1)} %pad_clamp_fusion), kind=kCustom, calls=%fused_computation.1 | custom fusion | bytes 12583424 | tf_op jit(solution)/shard_map/gather | solution.py:106
  167.7 6.6 %copy.43 = bf16[16,64,8,384]{3,2,0,1:T(8,128)(2,1)} copy(bf16[16,64,8,384]{3,2,1,0:T(8,128)(2,1)} %bitcast.66) | data formatting | bytes 12582912 | tf_op jit(solution)/shard_map/reshape | solution.py:109
  174.3 15.9 %all-to-all-start.2 = ((bf16[128,64,384]{2,0,1:T(8,128)(2,1)}), bf16[128,64,384]{2,0,1:T(8,128)(2,1)}, u32[]{:S(2)}, u32[]{:S(2)}) async-start(bf16[128,64,384]{2,0,1:T(8,128)(2,1)} %bitcast.65), calls=%async_computation.2 | async-start | bytes 12582912 | tf_op jit(solution)/shard_map/all_to_all | solution.py:108
  190.3 1.6 slice-done
  192.8 5.8 convolution_convert_fusion.1
  198.5 2.4 concatenate.16
  200.9 5.8 convolution_convert_fusion
  206.9 4.0 fusion.21
  210.9 117.9 %all-to-all-done.2 = bf16[128,64,384]{2,0,1:T(8,128)(2,1)} async-done(((bf16[128,64,384]{2,0,1:T(8,128)(2,1)}), bf16[128,64,384]{2,0,1:T(8,128)(2,1)}, u32[]{:S(2)}, u32[]{:S(2)}) %all-to-all-start.2) | async-done | bytes 6291488 | tf_op jit(solution)/shard_map/all_to_all | solution.py:108
  328.8 9.0 %copy.36 = bf16[64,128,1,384]{1,0,3,2:T(8,128)(2,1)} copy(bf16[64,128,1,384]{3,1,0,2:T(8,128)(2,1)} %bitcast.19) | data formatting | bytes 12582912 | tf_op jit(solution)/shard_map/all_to_all | solution.py:108
  337.8 10.3 %reshape.192 = bf16[8192,2,192]{0,2,1:T(8,128)(2,1)} reshape(bf16[64,128,1,384]{1,0,3,2:T(8,128)(2,1)} %copy.36) | data formatting | bytes 12582912 | tf_op jit(solution)/shard_map/reshape | solution.py:115
  348.1 120.6 %while.12 = (s32[]{:T(128)}, bf16[16,512,2,128]{1,3,2,0:T(8,128)(2,1)}, s32[16]{0:T(128)S(1)}, bf16[8448,2,128]{0,2,1:T(8,128)(2,1)}, s32[8448]{0:T(1024)S(1)}, ...) while((s32[]{:T(128)}, ...), condition=%wide.region_12.13_spmd, body=%wide.region_9.12_spmd.sunk | while | flops 510920704 | bytes 15042358 | solution.py:53
  349.4 1.8 fusion.45
  351.7 1.5 fusion.46
  353.2 2.4 fusion.47
  356.9 1.8 fusion.45
  359.2 1.5 fusion.46
  360.7 2.4 fusion.47
  364.4 1.8 fusion.45
  366.8 1.5 fusion.46
  368.3 2.4 fusion.47
  371.9 1.8 fusion.45
  374.3 1.5 fusion.46
  375.8 2.4 fusion.47
  379.4 1.8 fusion.45
  381.8 1.5 fusion.46
  383.3 2.4 fusion.47
  387.0 1.8 fusion.45
  389.3 1.5 fusion.46
  390.8 2.4 fusion.47
  394.5 1.8 fusion.45
  396.8 1.5 fusion.46
  398.3 2.4 fusion.47
  402.0 1.8 fusion.45
  404.4 1.5 fusion.46
  405.9 2.4 fusion.47
  409.5 1.8 fusion.45
  411.9 1.5 fusion.46
  413.4 2.4 fusion.47
  417.0 1.8 fusion.45
  419.4 1.5 fusion.46
  420.9 2.4 fusion.47
  424.6 1.8 fusion.45
  428.4 2.4 fusion.47
  432.1 1.8 fusion.45
  435.9 2.4 fusion.47
  439.6 1.8 fusion.45
  443.5 2.4 fusion.47
  447.1 1.8 fusion.45
  451.0 2.4 fusion.47
  454.6 1.8 fusion.45
  458.5 2.4 fusion.47
  462.2 1.8 fusion.45
  466.0 2.4 fusion.47
  468.7 6.5 %copy.38 = bf16[16,512,2,128]{1,0,3,2:T(8,128)(2,1)} copy(bf16[16,512,2,128]{1,3,2,0:T(8,128)(2,1)} %get-tuple-element.95) | data formatting | bytes 8388608 | tf_op jit(solution)/shard_map/while | solution.py:53
  475.2 7.5 %reshape_reshape.3 = bf16[64,128,1,256]{1,0,3,2:T(8,128)(2,1)} reshape(bf16[16,512,2,128]{1,0,3,2:T(8,128)(2,1)} %copy.38) | data formatting | bytes 8388608 | tf_op jit(solution)/shard_map/reshape;reshape | solution.py:133
  482.7 4.9 copy.39
  487.6 103.0 %all_to_all.55 = bf16[64,128,1,256]{1,3,2,0:T(8,128)(2,1)} all-to-all(bf16[64,128,1,256]{1,3,2,0:T(8,128)(2,1)S(1)} %copy.39), channel_id=1, replica_groups=mesh['rows'=4,'seq'=64] {'seq'}, dimensions={0} | all-to-all | bytes 8388608 | tf_op jit(solution)/shard_map/all_to_all | solution.py:132
  590.5 6.4 %copy.40 = bf16[128,16384]{1,0:T(8,128)(2,1)} copy(bf16[128,16384]{0,1:T(8,128)(2,1)} %bitcast.67) | data formatting | bytes 8388608 | tf_op jit(solution)/shard_map/reshape | solution.py:139
  (138 shorter events, 34.7 us)
Async XLA Ops:
  6.5 186.2 %copy-start = (bf16[512,256]{1,0:T(8,128)(2,1)S(1)}, bf16[512,256]{1,0:T(8,128)(2,1)}, u32[]{:S(2)}) copy-start(bf16[512,256]{1,0:T(8,128)(2,1)} %param.15) | copy-start | bytes 786436
  11.2 10.5 %all-to-all-start = ((bf16[4,48,576]{2,1,0:T(8,128)(2,1)}), bf16[4,48,576]{2,1,0:T(8,128)(2,1)S(1)}, u32[]{:S(2)}, u32[]{:S(2)}) async-start(bf16[4,48,576]{2,1,0:T(8,128)(2,1)} %bitcast.7), calls=%async_computation | async-start | bytes 491520 | tf_op jit(solution)/shard_map/all_to_all | solution.py:60
  16.3 174.1 %all-gather.2.cloned.1.call-start = ((), (), s32[]{:S(2)}) async-start(), calls=%async_computation.4 | async-start | bytes 10649600 | tf_op jit(solution)/shard_map/all_gather | solution.py:117
  174.3 16.0 %copy-start.2 = (s32[1,8192]{1,0:T(1,128)S(1)}, s32[1,8192]{1,0:T(1,128)}, u32[]{:S(2)}) copy-start(s32[1,8192]{1,0:T(1,128)} %param.12) | copy-start | bytes 98308
  174.3 154.5 %all-to-all-start.2 = ((bf16[128,64,384]{2,0,1:T(8,128)(2,1)}), bf16[128,64,384]{2,0,1:T(8,128)(2,1)}, u32[]{:S(2)}, u32[]{:S(2)}) async-start(bf16[128,64,384]{2,0,1:T(8,128)(2,1)} %bitcast.65), calls=%async_computation.2 | async-start | bytes 12582912 | tf_op jit(solution)/shard_map/all_to_all | solution.py:108
  190.3 1.6 slice-start
  198.5 2.4 copy-start.3
  487.6 109.3 %copy-start.1 = (bf16[512,256]{1,0:T(8,128)(2,1)S(1)}, bf16[512,256]{1,0:T(8,128)(2,1)}, u32[]{:S(2)}) copy-start(bf16[512,256]{1,0:T(8,128)(2,1)} %param.15) | copy-start | bytes 786436
Sparse Core Ops, SparseCore 0:
  24.3 89.1 all-gather.1
where the time goes:
time: 616 us; the launch traced here: 604 us
  blocking collectives  213 us (35%)
  waiting for transfers between devices  122 us (20%)
  local copies, waits for them, and re-layouts  106 us (17%)
  matrix products  79.5 us (13%)
  other arithmetic  38 us (6%)
  starting transfers between devices  21 us (3%)
  between operations  14 us (2%)
  loops' own time  10.6 us (2%)
    all_to_all x1, waiting for transfers between devices, local(): lax.all_to_all(packed_query.reshape(num_tokens, group_count, local_heads...  118 us
    all_to_all x1, blocking collectives, reshard_both(): lax.all_to_all(query_buffer, 'rows', split_axis=0, concat_axis=0, tiled=T...  110 us
    all_to_all x1, blocking collectives, local(): lax.all_to_all(head_out.reshape(group_count, num_tokens, 1, local_heads *...  103 us
    dot_general x16, matrix products, one_block(): jnp.einsum('hqk,khd->qhd', weights, value_block, preferred_element_type=j...  39 us
    dot_general x16, matrix products, one_block(): jnp.einsum('qhd,khd->hqk', query_block, key_block, preferred_element_type...  29 us
    sub x16, other arithmetic, one_block(): weights = jnp.exp(scores - top_score)  23.9 us
    gather x1, local copies, waits for them, and re-layouts, local(): packed_query = query_in[take_index]  17.5 us
    scatter x1, local copies, waits for them, and re-layouts, local(): query_buffer = jnp.zeros((num_rows * capacity, rollout_query.shape[1]), j...  16 us
  transfers between devices with their start and end apart: 3, of which 2 were waited for; matrix products, arithmetic and copies ran while one was open for 10% of the time, Pallas kernels for 0%

commit v1 on v0

v1 whole, which is shorter than its diff:
```python
import math

import jax
import jax.numpy as jnp
from jax import lax
from jax.experimental import pallas as pl
from jax.experimental.pallas import tpu as pltpu
from jax.sharding import PartitionSpec as P

HEADS = 128
QK_NOPE = 128
QK_ROPE = 64
V_HEAD = 128
LATENT = 512
TOK = 128
ROWS = 4
X_CHIPS = 4
Z_CHIPS = 8
STEPS = 8
LOOK = 8
PAIR_Q = 2 * (QK_NOPE + QK_ROPE)
PAIR_V = 2 * V_HEAD
WIDE = LATENT + 2 * QK_ROPE
SPAN = 3 * TOK
WINDOW = 4 * TOK
SCALE = math.log2(math.e) / math.sqrt(QK_NOPE + QK_ROPE)
MESH = pl.DeviceIdType.MESH
F32 = jnp.float32
BF16 = jnp.bfloat16


def kernel(
    q_ref, lat_ref, tgt_ref, seg_ref, gain_ref, ku_ref, vu_ref, out_ref,
    gath, tgts, segs, lat4, perm, bias, rope_hi, w_own, w_buf, q_buf, o_buf, ka_buf, kb_buf, v_buf,
    gath_s, gath_r, seg_s, seg_r, tgt_s, tgt_r, halo_s, halo_r,
    w_s, w_r, q_s, q_r, o_s, o_r,
):
    r = lax.axis_index("rows")
    s = lax.axis_index("seq")
    c = lax.rem(s, 2)
    chip = s // 2
    x = lax.rem(chip, X_CHIPS)
    z = chip // X_CHIPS

    def at(row, zz, xx, core):
        return (row, (zz * X_CHIPS + xx) * 2 + core)

    sib = (r, chip * 2 + (1 - c))
    next_chip = (r, lax.rem(chip + 1, X_CHIPS * Z_CHIPS) * 2 + c)
    prev_chip = (r, lax.rem(chip + X_CHIPS * Z_CHIPS - 1, X_CHIPS * Z_CHIPS) * 2 + c)
    z_up = at(r, lax.rem(z + 1, Z_CHIPS), x, c)
    z_down = at(r, lax.rem(z + Z_CHIPS - 1, Z_CHIPS), x, c)
    x_to = at(r, z, lax.rem(x + X_CHIPS - r, X_CHIPS), c)
    x_from = at(r, z, lax.rem(x + r, X_CHIPS), c)
    group = [
        (dr, dc, lax.rem(r + dr, ROWS), lax.rem(c + dc, 2))
        for dr in range(ROWS)
        for dc in range(2)
        if (dr, dc) != (0, 0)
    ]

    barrier = pltpu.get_barrier_semaphore()
    for _, _, row, core in group:
        pl.semaphore_signal(barrier, 1, device_id=at(row, z, x, core), device_id_type=MESH)
    for peer in (next_chip, prev_chip, z_up, z_down):
        pl.semaphore_signal(barrier, 1, device_id=peer, device_id_type=MESH)

    @pl.when(r != 0)
    def _():
        for peer in (x_to, x_from):
            pl.semaphore_signal(barrier, 1, device_id=peer, device_id_type=MESH)

    def source_seq(t, row, core):
        up = lax.rem(t, 2)
        off = up * ((t + 1) // 2) - (1 - up) * (t // 2)
        z_src = lax.rem(z + off + Z_CHIPS, Z_CHIPS)
        return z_src * (2 * X_CHIPS) + lax.rem(row + x, X_CHIPS) * 2 + core

    raw = lat_ref[:, :LATENT].astype(F32)
    inverse = lax.rsqrt(jnp.mean(raw * raw, axis=1, keepdims=True) + 1e-06)
    gath[r, :, :LATENT] = (raw * inverse * gain_ref[...]).astype(BF16)
    gath[r, :, LATENT:] = jnp.concatenate(
        [lat_ref[:, LATENT:], jnp.zeros((TOK, QK_ROPE), BF16)], axis=1
    )
    w_own[:, :128] = ku_ref[:, :128]
    w_own[:, 128:256] = pltpu.roll(ku_ref[:, 128:].astype(F32), 64, 1).astype(BF16)
    w_own[:, 256:] = vu_ref[...]
    tgts[c] = jnp.concatenate([tgt_ref[i : i + 1, :] for i in range(ROWS)], axis=1)
    before = pl.multiple_of(jnp.maximum(chip - 1, 0) * 2 * TOK, 2 * TOK)
    segs[r, :, : 2 * TOK] = seg_ref[:, pl.ds(before, 2 * TOK)]
    segs[r, :, 2 * TOK :] = seg_ref[:, pl.ds(pl.multiple_of(chip * 2 * TOK, 2 * TOK), 2 * TOK)]

    @pl.when(r != 0)
    def _():
        pl.semaphore_wait(barrier, 13)

    @pl.when(r == 0)
    def _():
        pl.semaphore_wait(barrier, 11)

    def remote(src, dst, send, recv, peer):
        return pltpu.make_async_remote_copy(
            src_ref=src, dst_ref=dst, send_sem=send, recv_sem=recv,
            device_id=peer, device_id_type=MESH,
        )

    def lat_copy(dr):
        peer = at(lax.rem(r + dr, ROWS), z, x, c)
        return remote(gath.at[r], gath.at[r], gath_s.at[dr - 1], gath_r.at[dr - 1], peer)

    def seg_copy(dr):
        peer = at(lax.rem(r + dr, ROWS), z, x, c)
        return remote(segs.at[r], segs.at[r], seg_s.at[dr - 1], seg_r.at[dr - 1], peer)

    tgt_copy = remote(tgts.at[c], tgts.at[c], tgt_s, tgt_r, sib)
    for dr in (1, 3, 2):
        lat_copy(dr).start()
    tgt_copy.start()
    for dr in (1, 3, 2):
        seg_copy(dr).start()

    w_first = remote(w_own, w_buf.at[0], w_s.at[0], w_r.at[0], x_to)

    @pl.when(r != 0)
    def _():
        w_first.start()

    @pl.when(r == 0)
    def _():
        pltpu.make_async_copy(w_own, w_buf.at[0], w_r.at[0]).start()

    def w_wait(t):
        pltpu.make_async_copy(w_buf.at[t], w_buf.at[t], w_r.at[t]).wait()

    def w_copy(src, dst, peer):
        return remote(w_buf.at[src], w_buf.at[dst], w_s.at[dst], w_r.at[dst], peer)

    def q_copy(t, i):
        dr, dc, row, core = group[i]
        cols = pl.ds(pl.multiple_of(source_seq(t, row, core) * PAIR_Q, 128), PAIR_Q)
        return remote(
            q_ref.at[:, cols], q_buf.at[t, c, r], q_s.at[t, i], q_r.at[t], at(row, z, x, core)
        )

    def q_start(t):
        for i in (0, 1, 5, 2, 6, 3, 4):
            q_copy(t, i).start()
        cols = pl.ds(pl.multiple_of(source_seq(t, r, c) * PAIR_Q, 128), PAIR_Q)
        pltpu.make_async_copy(q_ref.at[:, cols], q_buf.at[t, c, r], q_r.at[t]).start()

    def q_first(t, carry):
        q_start(t)
        return carry

    lax.fori_loop(0, LOOK, q_first, 0)

    def fill_perm(core):
        targets = tgts[core]
        row_ids = lax.broadcasted_iota(jnp.int32, (8, WINDOW), 0)
        hot = (targets == row_ids).astype(F32)
        earlier = (
            lax.broadcasted_iota(jnp.int32, (WINDOW, WINDOW), 0)
            < lax.broadcasted_iota(jnp.int32, (WINDOW, WINDOW), 1)
        ).astype(F32)
        counts = jnp.dot(
            hot.astype(BF16), earlier.astype(BF16), preferred_element_type=F32
        )
        rank = jnp.sum(hot * counts, axis=0, keepdims=True).astype(jnp.int32)
        slot = targets * TOK + rank
        perm[core] = (
            lax.broadcasted_iota(jnp.int32, (WINDOW, WINDOW), 0) == slot
        ).astype(F32).astype(BF16)

    fill_perm(c)
    for dr in (1, 3, 2):
        lat_copy(dr).wait_recv()
    lat4[2 + c] = jnp.dot(
        perm[c], gath[...].reshape(WINDOW, WIDE), preferred_element_type=F32
    ).astype(BF16)
    own_next = remote(lat4.at[2 + c], lat4.at[c], halo_s.at[0], halo_r.at[0], next_chip)
    own_sib = remote(lat4.at[2 + c], lat4.at[2 + c], halo_s.at[1], halo_r.at[1], sib)
    fwd_sib = remote(lat4.at[c], lat4.at[c], halo_s.at[2], halo_r.at[2], sib)
    own_next.start()
    own_sib.start()

    w_wait(0)
    w_copy(0, 1, z_down).start()
    w_copy(0, 2, z_up).start()

    tgt_copy.wait_recv()
    fill_perm(1 - c)
    for dr in (1, 3, 2):
        seg_copy(dr).wait_recv()

    eye = lax.broadcasted_iota(jnp.int32, (TOK, TOK), 0) == lax.broadcasted_iota(
        jnp.int32, (TOK, TOK), 1
    )
    for core in range(2):
        key_pos = lax.broadcasted_iota(jnp.int32, (TOK, SPAN), 1)
        query_pos = lax.broadcasted_iota(jnp.int32, (TOK, SPAN), 0) + 2 * TOK
        there = (key_pos + core * TOK + chip * 1024) >= 2 * TOK
        causal = (key_pos <= query_pos) & there
        for row in range(ROWS):
            seg = segs[row].astype(F32)
            seg_k = seg[:, core * TOK : core * TOK + SPAN]
            seg_q = jnp.sum(
                jnp.where(eye, seg[:, (2 + core) * TOK : (3 + core) * TOK], 0.0),
                axis=1,
                keepdims=True,
            )
            bias[core, row] = jnp.where((seg_q == seg_k) & causal, 0.0, -1e30)

    own_next.wait_recv()
    fwd_sib.start()
    own_sib.wait_recv()
    fwd_sib.wait_recv()
    for row in range(ROWS):
        tile = lat4[:, row * TOK : (row + 1) * TOK, LATENT:].reshape(WINDOW, 128)
        rope_hi[row] = pltpu.roll(tile.astype(F32), 64, 1)

    low = lax.broadcasted_iota(jnp.int32, (WINDOW, 128), 1) < 64

    def o_copy(t, row, core):
        cols = pl.ds(pl.multiple_of(source_seq(t, r, c) * PAIR_V, 128), PAIR_V)
        return remote(
            o_buf.at[t, core, row], out_ref.at[:, cols], o_s.at[t, core, row], o_r.at[t],
            at(row, z, x, core),
        )

    def step(t, carry):
        @pl.when(t > 0)
        def _():
            w_wait(t)

        @pl.when((t > 0) & (t < STEPS - 2) & (lax.rem(t, 2) == 1))
        def _():
            w_copy(t, t + 2, z_down).start()

        @pl.when((t > 0) & (t < STEPS - 2) & (lax.rem(t, 2) == 0))
        def _():
            w_copy(t, t + 2, z_up).start()

        @pl.when(t + LOOK < STEPS)
        def _():
            q_start(t + LOOK)

        pltpu.make_async_copy(q_buf.at[t], q_buf.at[t], q_r.at[t]).wait()

        def one_row(row, carry):
            rows = pl.ds(pl.multiple_of(row * TOK, TOK), TOK)
            lat = lat4[:, rows, :].reshape(WINDOW, WIDE)
            kv = jnp.dot(lat[:, :LATENT], w_buf[t], preferred_element_type=F32)
            ka_buf[:, :128] = kv[:, :128].astype(BF16)
            ka_buf[:, 128:] = lat[:, LATENT:]
            kb = kv[:, 128:256]
            kb_buf[:, :128] = jnp.where(low, 0.0, kb).astype(BF16)
            kb_buf[:, 128:] = jnp.where(low, kb, rope_hi[row]).astype(BF16)
            v_buf[...] = kv[:, 256:].astype(BF16)
            for core in range(2):
                q = jnp.dot(
                    perm[core, rows, :],
                    q_buf[t, core].reshape(WINDOW, PAIR_Q),
                    preferred_element_type=F32,
                ).astype(BF16)
                keys = slice(core * TOK, core * TOK + SPAN)
                for head, k_buf in ((0, ka_buf), (1, kb_buf)):
                    scores = lax.dot_general(
                        q[:, head * 128 : head * 128 + 256], k_buf[keys, :],
                        (((1,), (1,)), ((), ())), preferred_element_type=F32,
                    )
                    scores = scores * SCALE + bias[core, row]
                    top = jnp.max(scores, axis=1, keepdims=True)
                    weights = jnp.exp2(scores - top)
                    total = jnp.sum(weights, axis=1, keepdims=True)
                    probs = (weights * (1.0 / total)).astype(BF16)
                    mixed = jnp.dot(
                        probs, v_buf[keys, head * 128 : (head + 1) * 128],
                        preferred_element_type=F32,
                    )
                    o_buf[t, core, row, :, head * 128 : (head + 1) * 128] = mixed.astype(BF16)
                own = (row == r) & (c == core)

                @pl.when(jnp.logical_not(own))
                def _():
                    o_copy(t, row, core).start()

                @pl.when(own)
                def _():
                    cols = pl.ds(pl.multiple_of(source_seq(t, r, c) * PAIR_V, 128), PAIR_V)
                    pltpu.make_async_copy(
                        o_buf.at[t, core, row], out_ref.at[:, cols], o_r.at[t]
                    ).start()
            return carry

        lax.fori_loop(0, ROWS, one_row, 0)
        return carry

    lax.fori_loop(0, STEPS, step, 0)

    for dr in (1, 3, 2):
        lat_copy(dr).wait_send()
        seg_copy(dr).wait_send()
    tgt_copy.wait_send()
    own_next.wait_send()
    own_sib.wait_send()
    fwd_sib.wait_send()

    @pl.when(r != 0)
    def _():
        w_first.wait_send()

    def w_drain(t, carry):
        w_copy(0, t, z_down).wait_send()
        return carry

    lax.fori_loop(1, STEPS, w_drain, 0)

    def drain(t, carry):
        for i in range(7):
            q_copy(t, i).wait_send()
        for dr, dc, row, core in group:
            o_copy(t, row, core).wait_send()
        done = out_ref.at[:, pl.ds(pl.multiple_of(t * 8 * PAIR_V, 128), 8 * PAIR_V)]
        pltpu.make_async_copy(done, done, o_r.at[t]).wait()
        return carry

    lax.fori_loop(0, STEPS, drain, 0)


def local(rollout_query, rollout_latent, trainer_row, segment_ids, kv_gain, key_up, value_up):
    vmem = pl.BlockSpec(memory_space=pltpu.VMEM)
    hbm = pl.BlockSpec(memory_space=pl.ANY)
    dma = pltpu.SemaphoreType.DMA
    return pl.pallas_call(
        kernel,
        out_shape=jax.ShapeDtypeStruct((TOK, HEADS * V_HEAD), BF16),
        in_specs=[hbm] + [vmem] * 6,
        out_specs=hbm,
        scratch_shapes=[
            pltpu.VMEM((ROWS, TOK, WIDE), BF16),
            pltpu.VMEM((2, 1, WINDOW), jnp.int32),
            pltpu.VMEM((ROWS, 1, WINDOW), jnp.int32),
            pltpu.VMEM((4, WINDOW, WIDE), BF16),
            pltpu.VMEM((2, WINDOW, WINDOW), BF16),
            pltpu.VMEM((2, ROWS, TOK, SPAN), F32),
            pltpu.VMEM((ROWS, WINDOW, 128), F32),
            pltpu.VMEM((LATENT, 512), BF16),
            pltpu.VMEM((STEPS, LATENT, 512), BF16),
            pltpu.VMEM((STEPS, 2, ROWS, TOK, PAIR_Q), BF16),
            pltpu.VMEM((STEPS, 2, ROWS, TOK, PAIR_V), BF16),
            pltpu.VMEM((WINDOW, 256), BF16),
            pltpu.VMEM((WINDOW, 256), BF16),
            pltpu.VMEM((WINDOW, 256), BF16),
            dma((3,)), dma((3,)), dma((3,)), dma((3,)), dma, dma, dma((3,)), dma((3,)),
            dma((STEPS,)), dma((STEPS,)), dma((STEPS, 7)), dma((STEPS,)), dma((STEPS, 2, ROWS)),
            dma((STEPS,)),
        ],
        compiler_params=pltpu.CompilerParams(
            collective_id=0, has_side_effects=True, vmem_limit_bytes=56 << 20
        ),
        cost_estimate=pl.CostEstimate(
            flops=18_000_000_000, bytes_accessed=24_000_000, transcendentals=6_500_000
        ),
    )(
        rollout_query, rollout_latent, trainer_row, segment_ids, kv_gain.reshape(1, LATENT),
        key_up, value_up,
    )


def solution(mesh):
    placed = (
        P(("rows", "seq"), None),
        P(("rows", "seq"), None),
        P(None, "seq"),
        P("rows", None),
        P(),
        P(None, "seq"),
        P(None, "seq"),
    )
    return jax.shard_map(
        local, mesh=mesh, in_specs=placed, out_specs=P(("rows", "seq"), None), check_vma=False
    )
```

time: 616 us -> 141 us (0.23); the launches traced: 604 us -> 141 us
  blocking collectives: 213 us -> 0 us
  Pallas kernels: 0 us -> 135 us
  waiting for transfers between devices: 122 us -> 0 us
  local copies, waits for them, and re-layouts: 106 us -> 6.28 us
  matrix products: 79.5 us -> 0 us
  other arithmetic: 38 us -> 0 us
  starting transfers between devices: 21 us -> 0 us
  between operations: 14 us -> 0.01 us
  loops' own time: 10.6 us -> 0 us
    all_to_all x2 -> x0, blocking collectives: 213 us -> none  [the longest x1 110 us: reshard_both(): lax.all_to_all(query_buffer, 'rows', split_axis=0, concat_axis=0, tiled=T...]
    pallas_call x0 -> x1, Pallas kernels: none -> 135 us  [local(): pl.pallas_call(kernel, out_shape=jax.ShapeDtypeStruct((TOK, HEADS * V_HEA...]
    all_to_all x2 -> x0, waiting for transfers between devices: 122 us -> none  [the longest x1 118 us: local(): lax.all_to_all(packed_query.reshape(num_tokens, group_count, local_heads...]
    dot_general x34 -> x0, matrix products: 79.5 us -> none  [the longest x16 39 us: one_block(): jnp.einsum('hqk,khd->qhd', weights, value_block, preferred_element_type=j...]
    sub x17 -> x0, other arithmetic: 23.9 us -> none  [the longest x16 23.9 us: one_block(): weights = jnp.exp(scores - top_score)]
    reshape x3 -> x0, local copies, waits for them, and re-layouts: 23.3 us -> none  [the longest x1 10.3 us: local(): head_query = head_query.reshape(row_length, local_heads, head_width)]
    all_to_all x2 -> x0, starting transfers between devices: 21 us -> none  [the longest x1 15.9 us: local(): lax.all_to_all(packed_query.reshape(num_tokens, group_count, local_heads...]
    gather x2 -> x0, local copies, waits for them, and re-layouts: 18.4 us -> none  [the longest x1 17.5 us: local(): packed_query = query_in[take_index]]
  transfers between devices with their start and end apart: 3 -> 0, of which waited for: 2 -> 0; matrix products, arithmetic and copies ran while one was open for 10% -> 0% of each run, Pallas kernels for 0% -> 0%
where the time goes in v1:
time: 141 us
  Pallas kernels  135 us (96%)
  local copies, waits for them, and re-layouts  6.28 us (4%)
    pallas_call x1, Pallas kernels, local(): pl.pallas_call(kernel, out_shape=jax.ShapeDtypeStruct((TOK, HEADS * V_HEA...  135 us
    unnamed x2, local copies, waits for them, and re-layouts  6.28 us

profile of v1, /device:TPU:1, one launch (start us, length us, event | category | flops | bytes accessed | tf_op | source)
XLA Modules:
  0.0 140.8 jit_solution(8135954245358299016)
XLA Ops:
  0.0 1.7 %copy.8.lat_ref = bf16[128,576]{1,0:T(8,128)(2,1)} copy(bf16[128,576]{0,1:T(8,128)(2,1)} %param.8) | data formatting | bytes 294912 | tf_op args[1]
  1.7 134.6 %shard_map.73 = bf16[128,16384]{1,0:T(8,128)(2,1)} custom-call(bf16[128,24576]{1,0:T(8,128)(2,1)} %q_ref.1, bf16[128,576]{1,0:T(8,128)(2,1)} %copy.8.lat_ref, s32[4,128]{1,0:T(4,128)} %tgt_ref.1, s32[1,8192]{1,0:T(1,128)} %seg_ref.1, f32[1,512]{1,0:T(1,128)} %bitcast.1, bf16[512,256]{1,0:T(8,128)(2,1)} %ku_ref.1, bf16[512,256]{1,0:T(8,128)(2,1)} %vu_ref.1), custom_call_target="tpu_custom_call" | custom-call | flops 17999998976 | bytes 24000000 | tf_op jit(solution)/shard_map/pallas_call | solution.py:334
  136.3 4.6 %copy.10 = bf16[128,16384]{1,0:T(8,128)(2,1)} copy(bf16[128,16384]{1,0:T(8,128)(2,1)} %shard_map.73) | data formatting | bytes 8388608
